TPU v7x, 768 devices: a whole 4x8x12 slice. The times are simulated.
768 devices in a mesh: fsdp: 96 (over z_hi, x, y), tensor: 8 (over z_lo, core).
Axes of the slice: x: 4, y: 8, z: 12 (z_hi: 3, z_lo: 4; z = z_hi * 4 + z_lo), core: 2. Of those that a mesh axis runs over, the one named last changes fastest.
Arguments:
- out_grad: bfloat16 [98304, 2048], P(('fsdp', 'tensor')), may hold values from -6 to 6
- hidden: bfloat16 [98304, 3072], P('fsdp', 'tensor'), may hold values from -6 to 6
- segments: int32 [96, 1024], P('fsdp'), may hold values from 0 to 7, never falling along the last dimension, each value on 1 to 512 neighbouring positions
- master: float32 [3072, 2048], P(('tensor', 'fsdp')), may hold values from -0.078125 to 0.078125
- moment_one: float32 [3072, 2048], P(('tensor', 'fsdp')), may hold values from -0.15625 to 0.15625
- moment_two: float32 [3072, 2048], P(('tensor', 'fsdp')), may hold values from 1e-05 to 0.001
- step_count: int32 [], replicated, may hold values from 1 to 40
- layer_one: bfloat16 [3072, 2048], P(('tensor', 'fsdp')), may hold values from -0.078125 to 0.078125
Outputs:
- hidden_grad: bfloat16 [98304, 3072], P('fsdp', 'tensor')
- new_master: float32 [3072, 2048], P(('tensor', 'fsdp'))
- new_moment_one: float32 [3072, 2048], P(('tensor', 'fsdp'))
- new_moment_two: float32 [3072, 2048], P(('tensor', 'fsdp'))
- update: float32 [3072, 2048], P(('tensor', 'fsdp'))
- layer_one_rows: bfloat16 [3072, 2048], P('tensor')
Inputs may be any that keep to these rules, and one draw needn't show every extreme that they name: `segments`: within a row document numbers never fall and every document has at least one token; some document has exactly 512 tokens.
All inputs are finite; a program needn't handle non-finite values.
Results may differ from a plain program's by a relative error of at most 0.0055.
Values may be sent and summed in bfloat16 or wider, within the bound.
No kernel may reach another device: no remote copies, remote signals or barrier semaphores. Data moves between devices by JAX's collectives and lax.ppermute only.
A program may use at most 64 MiB of HBM per device.

v0:
```python
import jax
import jax.numpy as jnp
from jax import lax
from jax.sharding import PartitionSpec as P

DOCS = 8


def per_device(out_grad, hidden, segments, master, moment_one, moment_two, step_count, layer_one):
    n_fsdp = lax.axis_size("fsdp")
    tok_dev = hidden.shape[0]
    all_tokens = tok_dev * n_fsdp
    seg_row = segments[0]
    same_doc = (seg_row[:, None] == seg_row[None, :]).astype(jnp.float32)
    doc_len = jnp.sum(same_doc, axis=1)
    weight = tok_dev / DOCS / doc_len
    rounded = master.astype(jnp.bfloat16)
    last_full = lax.all_gather(rounded, "fsdp", axis=0, tiled=True)
    full_grads = lax.all_gather(out_grad, "tensor", axis=0, tiled=True)
    scaled = (full_grads.astype(jnp.float32) * weight[:, None]).astype(jnp.bfloat16)
    grad_local = lax.dot_general(
        hidden, scaled, (((0,), (0,)), ((), ())), preferred_element_type=jnp.float32
    )
    gradient = lax.psum_scatter(grad_local, "fsdp", scatter_dimension=0, tiled=True)
    hidden_grad = lax.dot_general(
        scaled, last_full, (((1,), (1,)), ((), ())), preferred_element_type=jnp.float32
    )
    gradient = gradient / all_tokens
    new_moment_one = 0.9 * moment_one + 0.1 * gradient
    new_moment_two = 0.95 * moment_two + 0.05 * gradient * gradient
    step_float = step_count.astype(jnp.float32)
    first_fix = 1.0 - jnp.power(jnp.float32(0.9), step_float)
    second_fix = 1.0 - jnp.power(jnp.float32(0.95), step_float)
    update = (
        new_moment_one / first_fix / (jnp.sqrt(new_moment_two / second_fix) + 1e-08) + 0.1 * master
    )
    new_master = master - 0.00015 * update
    first_full = lax.all_gather(layer_one, "fsdp", axis=0, tiled=True)
    return (
        hidden_grad.astype(jnp.bfloat16),
        new_master,
        new_moment_one,
        new_moment_two,
        update,
        first_full,
    )


def solution(mesh):
    in_specs = (
        P(("fsdp", "tensor"), None),
        P("fsdp", "tensor"),
        P("fsdp", None),
        P(("tensor", "fsdp"), None),
        P(("tensor", "fsdp"), None),
        P(("tensor", "fsdp"), None),
        P(),
        P(("tensor", "fsdp"), None),
    )
    out_specs = (
        P("fsdp", "tensor"),
        P(("tensor", "fsdp"), None),
        P(("tensor", "fsdp"), None),
        P(("tensor", "fsdp"), None),
        P(("tensor", "fsdp"), None),
        P("tensor", None),
    )
    return jax.shard_map(
        per_device, mesh=mesh, in_specs=in_specs, out_specs=out_specs, check_vma=False
    )
```

profile of v0, /device:TPU:6, one launch (start us, length us, event | category | flops | bytes accessed | tf_op | source)
XLA Modules:
  0.0 1681.0 jit_solution(9048304465524085807)
XLA Ops:
  7.2 0.0 copy-start
  7.2 0.0 all-gather.6.cloned.1.call-start
  7.2 0.7 all-gather.6.cloned.1.call-update
  7.9 0.0 all-reduce.3.cloned.1.call-start
  8.0 1.3 convert_reduce_fusion
  9.3 68.3 %all-gather.6.cloned.1.call-done = bf16[1024,2048]{1,0:T(8,128)(2,1)} async-done(((bf16[128,2048]{1,0:T(8,128)(2,1)}), bf16[1024,2048]{1,0:T(8,128)(2,1)}) %all-gather.6.cloned.1.call-update) | async-done | bytes 4194320 | tf_op jit(solution)/shard_map/all_gather | solution.py:19
  77.6 6.4 convolution_bitcast_fusion
  84.0 0.0 all-reduce.3.cloned.1.call-update
  84.0 0.0 all-gather.10.cloned.1.call-start
  84.1 0.7 all-gather.10.cloned.1.call-update
  84.8 0.0 all-gather.8.cloned.1.call-start
  85.5 1.3 dynamic-slice
  87.5 1246.2 %all-reduce.3.cloned.1.call-done = f32[384,2048]{0,1:T(8,128)} async-done(((f32[384,2048]{0,1:T(8,128)}), f32[384,2048]{0,1:T(8,128)}) %all-reduce.3.cloned.1.call-update) | async-done | bytes 3145744
  1333.7 1.6 constant_dynamic-slice_fusion
  1335.2 0.3 copy.47
  1335.6 0.0 copy-done.2
  1335.6 0.0 copy-done.3
  1335.6 0.7 multiply_subtract_fusion
  1336.3 0.0 all-gather.8.cloned.1.call-update
  1336.3 174.2 %all-gather.10.cloned.1.call-done = bf16[96,4,2048]{2,1,0:T(4,128)(2,1)} async-done(((bf16[1,4,2048]{2,1,0:T(4,128)(2,1)}), bf16[96,4,2048]{2,1,0:T(4,128)(2,1)}) %all-gather.10.cloned.1.call-update) | async-done | bytes 1572880 | tf_op jit(solution)/shard_map/all_gather | solution.py:38
  1510.5 3.5 reshape.19
  1514.0 152.7 %all-gather.8.cloned.1.call-done = bf16[96,4,2048]{2,1,0:T(4,128)(2,1)} async-done(((bf16[1,4,2048]{2,1,0:T(4,128)(2,1)}), bf16[96,4,2048]{2,1,0:T(4,128)(2,1)}) %all-gather.8.cloned.1.call-update) | async-done | bytes 1572880 | tf_op jit(solution)/shard_map/all_gather | solution.py:18
  1666.6 2.3 reshape.17
  1669.0 5.5 fusion.1
  (6 shorter events, 0.0 us)
Async XLA Ops:
  7.2 70.4 %copy-start = (bf16[1024,384]{1,0:T(8,128)(2,1)S(1)}, bf16[1024,384]{1,0:T(8,128)(2,1)}, u32[]{:S(2)}) copy-start(bf16[1024,384]{1,0:T(8,128)(2,1)} %param.9) | copy-start | bytes 2359300
  7.2 70.4 %all-gather.6.cloned.1.call-start = ((), (), s32[]{:S(2)}) async-start(), calls=%async_computation | async-start | bytes 4718592 | tf_op jit(solution)/shard_map/all_gather | solution.py:19
  7.9 1325.8 %all-reduce.3.cloned.1.call-start = ((), (), s32[]{:S(2)}) async-start(), calls=%async_computation.3 | async-start | bytes 6291456
  84.0 1251.6 %copy-start.1 = (f32[4,2048]{1,0:T(4,128)S(1)}, f32[4,2048]{1,0:T(4,128)}, u32[]{:S(2)}) copy-start(f32[4,2048]{1,0:T(4,128)} %param.11) | copy-start | bytes 98308
  84.0 1251.6 %copy-start.2 = (f32[4,2048]{1,0:T(4,128)S(1)}, f32[4,2048]{1,0:T(4,128)}, u32[]{:S(2)}) copy-start(f32[4,2048]{1,0:T(4,128)} %param.13) | copy-start | bytes 98308
  84.0 1251.6 %copy-start.3 = (f32[4,2048]{1,0:T(4,128)S(1)}, f32[4,2048]{1,0:T(4,128)}, u32[]{:S(2)}) copy-start(f32[4,2048]{1,0:T(4,128)} %param.12) | copy-start | bytes 98308
  84.0 1426.5 %all-gather.10.cloned.1.call-start = ((), (), s32[]{:S(2)}) async-start(), calls=%async_computation.2 | async-start | bytes 1589248 | tf_op jit(solution)/shard_map/all_gather | solution.py:38
  84.8 1581.9 %all-gather.8.cloned.1.call-start = ((), (), s32[]{:S(2)}) async-start(), calls=%async_computation.1 | async-start | bytes 1589248 | tf_op jit(solution)/shard_map/all_gather | solution.py:18
Sparse Core Ops, SparseCore 0:
  10.4 67.1 all-gather.5
  84.1 1249.4 all-reduce.2
  1340.3 170.1 all-gather.9
  1517.5 149.0 all-gather.7
where the time goes:
time: 1680 us
  waiting for transfers between devices  1640 us (98%)
    unnamed x5, waiting for transfers between devices  1250 us
    all_gather x1, waiting for transfers between devices, per_device(): first_full = lax.all_gather(layer_one, 'fsdp', axis=0, tiled=True)  174 us
    all_gather x1, waiting for transfers between devices, per_device(): last_full = lax.all_gather(rounded, 'fsdp', axis=0, tiled=True)  153 us
    all_gather x1, waiting for transfers between devices, per_device(): full_grads = lax.all_gather(out_grad, 'tensor', axis=0, tiled=True)  68.3 us
  transfers between devices with their start and end apart: 4, of which 4 were waited for; matrix products, arithmetic and copies ran while one was open for 1% of the time, Pallas kernels for 0%

commit v1 on v0

v1 whole, which is shorter than its diff:
```python
import jax
import jax.numpy as jnp
from jax import lax
from jax.sharding import Mesh
from jax.sharding import PartitionSpec as P

DOCS = 8
BF = jnp.bfloat16
F32 = jnp.float32


def spread(block, axes, size):
    return lax.all_to_all(jnp.broadcast_to(block[None], (size,) + block.shape), axes, 0, 0)


def per_device(out_grad, hidden, segments, master, moment_one, moment_two, step_count, layer_one):
    n_zh, n_x, n_yh, n_yl = [lax.axis_size(a) for a in ("zh", "x", "yh", "yl")]
    n_y = n_yh * n_yl
    rows, width = master.shape
    tok_dev, units = hidden.shape
    all_tokens = tok_dev * n_zh * n_x * n_y

    with jax.named_scope("gather_grads"):
        full_grads = lax.all_gather(out_grad, ("zl", "c"), axis=0, tiled=True)

    with jax.named_scope("gather_weights"):
        pair = jnp.stack([master.astype(BF), layer_one])
        pair = spread(pair, "zh", n_zh)
        pair = spread(pair, ("yh", "yl"), n_y)
        pair = pair.transpose(2, 1, 0, 3, 4).reshape(2, n_zh * n_y * rows, width)
        last = spread(pair[0], "x", n_x)
        first = lax.all_gather(pair[1], "x", axis=0, tiled=False)

    def in_order(w):
        return w.reshape(n_x, n_zh, n_y * rows, width).transpose(1, 0, 2, 3).reshape(units, width)

    with jax.named_scope("weights_of_tokens"):
        seg_row = segments[0]
        same_doc = (seg_row[:, None] == seg_row[None, :]).astype(F32)
        doc_len = jnp.sum(same_doc, axis=1)
        weight = tok_dev / DOCS / doc_len
        scaled = (full_grads.astype(F32) * weight[:, None]).astype(BF)

    with jax.named_scope("unit_order"):
        place = jnp.arange(units, dtype=jnp.int32).reshape(n_zh, n_x, n_yh, n_yl, rows)
        place = place.transpose(1, 3, 0, 2, 4).reshape(units)
        pick = (jnp.arange(units, dtype=jnp.int32)[:, None] == place[None, :]).astype(BF)
        ordered = lax.dot_general(
            hidden, pick, (((1,), (0,)), ((), ())), preferred_element_type=F32
        ).astype(BF)

    with jax.named_scope("gradient"):
        grad_local = lax.dot_general(
            ordered, scaled, (((0,), (0,)), ((), ())), preferred_element_type=F32
        ).astype(BF)
        parts = lax.all_to_all(
            grad_local.reshape(n_x * n_yl, units // (n_x * n_yl), width), ("x", "yl"), 0, 0
        )
        part = jnp.sum(parts.astype(F32), axis=0).astype(BF)
        parts = lax.all_to_all(part.reshape(n_zh * n_yh, rows, width), ("zh", "yh"), 0, 0)
        gradient = jnp.sum(parts.astype(F32), axis=0)

    with jax.named_scope("hidden_grad"):
        hidden_grad = lax.dot_general(
            scaled, in_order(last), (((1,), (1,)), ((), ())), preferred_element_type=F32
        )

    with jax.named_scope("adamw"):
        gradient = gradient / all_tokens
        new_moment_one = 0.9 * moment_one + 0.1 * gradient
        new_moment_two = 0.95 * moment_two + 0.05 * gradient * gradient
        step_float = step_count.astype(F32)
        first_fix = 1.0 - jnp.power(F32(0.9), step_float)
        second_fix = 1.0 - jnp.power(F32(0.95), step_float)
        update = (
            new_moment_one / first_fix / (jnp.sqrt(new_moment_two / second_fix) + 1e-08)
            + 0.1 * master
        )
        new_master = master - 0.00015 * update
    return (
        hidden_grad.astype(BF),
        new_master,
        new_moment_one,
        new_moment_two,
        update,
        in_order(first),
    )


def solution(mesh):
    fine = Mesh(mesh.devices.reshape(3, 4, 4, 2, 4, 2), ("zh", "x", "yh", "yl", "zl", "c"))
    fsdp = ("zh", "x", "yh", "yl")
    tensor = ("zl", "c")
    in_specs = (
        P(fsdp + tensor, None),
        P(fsdp, tensor),
        P(fsdp, None),
        P(tensor + fsdp, None),
        P(tensor + fsdp, None),
        P(tensor + fsdp, None),
        P(),
        P(tensor + fsdp, None),
    )
    out_specs = (
        P(fsdp, tensor),
        P(tensor + fsdp, None),
        P(tensor + fsdp, None),
        P(tensor + fsdp, None),
        P(tensor + fsdp, None),
        P(tensor, None),
    )
    return jax.shard_map(
        per_device, mesh=fine, in_specs=in_specs, out_specs=out_specs, check_vma=False
    )
```

time: 1680 us -> 219 us (0.13)
  waiting for transfers between devices: 1640 us -> 83.2 us
  blocking collectives: 0 us -> 90.2 us
    unnamed x5 -> x2, waiting for transfers between devices: 1250 us -> 0.7 us
    all_gather x3 -> x2, waiting for transfers between devices: 395 us -> 68.2 us  [the longest x1 68.2 us: per_device(): full_grads = lax.all_gather(out_grad, ('zl', 'c'), axis=0, tiled=True)]
    all_to_all x0 -> x4, blocking collectives: none -> 90.2 us  [the longest x3 68.1 us: spread(): lax.all_to_all(jnp.broadcast_to(block[None], (size,) + block.shape), axes...]
  transfers between devices with their start and end apart: 4 -> 3, of which waited for: 4 -> 2; matrix products, arithmetic and copies ran while one was open for 1% -> 2% of each run, Pallas kernels for 0% -> 0%
where the time goes in v1:
time: 219 us; the launch traced here: 218 us
  blocking collectives  90.2 us (41%)
  waiting for transfers between devices  83.2 us (38%)
  between operations  14.9 us (7%)
  starting transfers between devices  12.6 us (6%)
  matrix products  8.86 us (4%)
  local copies, waits for them, and re-layouts  6.03 us (3%)
  other arithmetic  2.4 us (1%)
    all_gather x1, waiting for transfers between devices, per_device(): full_grads = lax.all_gather(out_grad, ('zl', 'c'), axis=0, tiled=True)  68.2 us
    all_to_all x3, blocking collectives, spread(): lax.all_to_all(jnp.broadcast_to(block[None], (size,) + block.shape), axes...  68.1 us
    all_to_all x1, blocking collectives, per_device(): lax.all_to_all(grad_local.reshape(n_x * n_yl, units // (n_x * n_yl), widt...  22.1 us
    all_to_all x1, waiting for transfers between devices, per_device(): lax.all_to_all(part.reshape(n_zh * n_yh, rows, width), ('zh', 'yh'), 0, 0)  14.3 us
    all_to_all x1, starting transfers between devices, per_device(): lax.all_to_all(part.reshape(n_zh * n_yh, rows, width), ('zh', 'yh'), 0, 0)  12.5 us
    dot_general x1, matrix products, per_device(): lax.dot_general(ordered, scaled, (((0,), (0,)), ((), ())), preferred_elem...  5.6 us
  transfers between devices with their start and end apart: 3, of which 2 were waited for; matrix products, arithmetic and copies ran while one was open for 2% of the time, Pallas kernels for 0%

profile of v1, /device:TPU:6, one launch (start us, length us, event | category | flops | bytes accessed | tf_op | source)
XLA Modules:
  0.0 218.2 jit_solution(17242473554286373118)
XLA Ops:
  7.2 0.7 all-gather.3.cloned.1.call-update
  7.9 0.1 reshape.140
  8.0 1.3 convert_reduce_fusion
  9.4 68.2 %all-gather.3.cloned.1.call-done = bf16[1024,2048]{1,0:T(8,128)(2,1)} async-done(((bf16[128,2048]{1,0:T(8,128)(2,1)}), bf16[1024,2048]{1,0:T(8,128)(2,1)}) %all-gather.3.cloned.1.call-update) | async-done | bytes 4194320 | tf_op jit(solution)/shard_map/gather_grads/all_gather | solution.py:24
  77.6 5.6 %convolution_convert_fusion = bf16[384,2048]{1,0:T(8,128)(2,1)} fusion(bf16[1024,2048]{1,0:T(8,128)(2,1)} %all-gather.3.cloned.1.call-done, f32[1024]{0:T(1024)S(1)} %broadcast_divide_fusion, bf16[1024,384]{1,0:T(8,128)(2,1)S(1)} %copy-done, s32[384]{0:T(512)S(1)} %reshape.140), kind=kOutput, calls=%fused_computation.2 | convolution fusion | flops 1920368640 | bytes 6559232 | tf_op jit(solution)/shard_map/gradient/dot_general | solution.py:53
  83.2 22.1 %all_to_all.25 = bf16[8,48,2048]{2,1,0:T(8,128)(2,1)S(1)} all-to-all(bf16[8,48,2048]{2,1,0:T(8,128)(2,1)} %bitcast.21), channel_id=1, replica_groups=mesh['zh'=3,'x'=4,'yh'=4,'yl'=2,'zl'=4,'c'=2] {'x','yl'}, dimensions={0} | all-to-all | bytes 3145728 | tf_op jit(solution)/shard_map/gradient/all_to_all | solution.py:56
  105.3 0.3 reduce_sum.31
  105.6 0.8 reshape.136
  106.3 12.5 %all-to-all-start.4 = ((bf16[12,4,2048]{2,1,0:T(4,128)(2,1)}), bf16[12,4,2048]{2,1,0:T(4,128)(2,1)S(1)}, u32[]{:S(2)}, u32[]{:S(2)}) async-start(bf16[12,4,2048]{2,1,0:T(4,128)(2,1)} %reshape.136), calls=%async_computation.4 | async-start | bytes 393216 | tf_op jit(solution)/shard_map/gradient/all_to_all | solution.py:60
  119.6 14.3 %all-to-all-done.4 = bf16[12,4,2048]{2,1,0:T(4,128)(2,1)S(1)} async-done(((bf16[12,4,2048]{2,1,0:T(4,128)(2,1)}), bf16[12,4,2048]{2,1,0:T(4,128)(2,1)S(1)}, u32[]{:S(2)}, u32[]{:S(2)}) %all-to-all-start.4) | async-done | bytes 196640 | tf_op jit(solution)/shard_map/gradient/all_to_all | solution.py:60
  134.0 0.7 multiply_subtract_fusion
  134.8 12.7 %all_to_all.26 = bf16[3,2,4,2048]{3,2,1,0:T(4,128)(2,1)S(1)} all-to-all(bf16[3,2,4,2048]{3,2,1,0:T(4,128)(2,1)S(1)} %broadcast_in_dim.8), channel_id=1, replica_groups=mesh['zh'=3,'x'=4,'yh'=4,'yl'=2,'zl'=4,'c'=2] {'zh'}, dimensions={0} | all-to-all | bytes 196608 | tf_op jit(solution)/shard_map/gather_weights/all_to_all | solution.py:13
  147.5 0.4 broadcast_in_dim.9
  147.9 20.3 %all_to_all.27 = bf16[8,3,2,4,2048]{4,3,1,2,0:T(4,128)(2,1)S(1)} all-to-all(bf16[8,3,2,4,2048]{4,3,1,2,0:T(4,128)(2,1)S(1)} %broadcast_in_dim.9), channel_id=1, replica_groups=mesh['zh'=3,'x'=4,'yh'=4,'yl'=2,'zl'=4,'c'=2] {'yh','yl'}, dimensions={0} | all-to-all | bytes 1572864 | tf_op jit(solution)/shard_map/gather_weights/all_to_all | solution.py:13
  168.2 0.3 fusion.7
  168.6 0.2 copy.24
  168.7 0.8 slice.12
  169.6 0.2 copy.22
  169.8 0.1 broadcast_in_dim.10
  169.9 0.2 broadcast_in_dim.11
  170.1 35.1 %all_to_all.28 = bf16[4,96,2048]{2,1,0:T(8,128)(2,1)S(1)} all-to-all(bf16[4,96,2048]{2,1,0:T(8,128)(2,1)S(1)} %broadcast_in_dim.11), channel_id=1, replica_groups=mesh['zh'=3,'x'=4,'yh'=4,'yl'=2,'zl'=4,'c'=2] {'x'}, dimensions={0} | all-to-all | bytes 3145728 | tf_op jit(solution)/shard_map/gather_weights/all_to_all | solution.py:13
  205.2 0.2 copy.23
  205.4 3.3 %fusion.1 = bf16[1024,384]{1,0:T(8,128)(2,1)} fusion(bf16[384,2048]{1,0:T(8,128)(2,1)S(1)} %bitcast.20, bf16[1024,2048]{1,0:T(8,128)(2,1)S(1)} %copy-done.5, f32[1024]{0:T(1024)S(1)} %broadcast_divide_fusion), kind=kOutput, calls=%fused_computation.4 | convolution fusion | flops 1617297408 | bytes 6557696 | tf_op jit(solution)/shard_map/hidden_grad/dot_general | solution.py:64
  208.6 2.7 %copy.25 = bf16[3,4,32,2048]{3,2,1,0:T(8,128)(2,1)} copy(bf16[3,4,32,2048]{3,2,0,1:T(8,128)(2,1)} %bitcast.18) | data formatting | bytes 3145728 | tf_op jit(solution)/shard_map/transpose | solution.py:35
  (22 shorter events, 0.3 us)
Async XLA Ops:
  7.2 70.4 %copy-start = (bf16[1024,384]{1,0:T(8,128)(2,1)S(1)}, bf16[1024,384]{1,0:T(8,128)(2,1)}, u32[]{:S(2)}) copy-start(bf16[1024,384]{1,0:T(8,128)(2,1)} %param.9) | copy-start | bytes 2359300
  7.2 70.4 %all-gather.3.cloned.1.call-start = ((), (), s32[]{:S(2)}) async-start(), calls=%async_computation.5 | async-start | bytes 4718592 | tf_op jit(solution)/shard_map/gather_grads/all_gather | solution.py:24
  83.2 50.8 %copy-start.1 = (f32[4,2048]{1,0:T(4,128)S(1)}, f32[4,2048]{1,0:T(4,128)}, u32[]{:S(2)}) copy-start(f32[4,2048]{1,0:T(4,128)} %param.11) | copy-start | bytes 98308
  83.2 50.8 %copy-start.2 = (f32[4,2048]{1,0:T(4,128)S(1)}, f32[4,2048]{1,0:T(4,128)}, u32[]{:S(2)}) copy-start(f32[4,2048]{1,0:T(4,128)} %param.13) | copy-start | bytes 98308
  83.2 50.8 %copy-start.3 = (f32[4,2048]{1,0:T(4,128)S(1)}, f32[4,2048]{1,0:T(4,128)}, u32[]{:S(2)}) copy-start(f32[4,2048]{1,0:T(4,128)} %param.12) | copy-start | bytes 98308
  83.2 51.5 %copy-start.4 = (bf16[4,2048]{1,0:T(4,128)(2,1)S(1)}, bf16[4,2048]{1,0:T(4,128)(2,1)}, u32[]{:S(2)}) copy-start(bf16[4,2048]{1,0:T(4,128)(2,1)} %param.15) | copy-start | bytes 49156
  106.3 27.6 %all-to-all-start.4 = ((bf16[12,4,2048]{2,1,0:T(4,128)(2,1)}), bf16[12,4,2048]{2,1,0:T(4,128)(2,1)S(1)}, u32[]{:S(2)}, u32[]{:S(2)}) async-start(bf16[12,4,2048]{2,1,0:T(4,128)(2,1)} %reshape.136), calls=%async_computation.4 | async-start | bytes 393216 | tf_op jit(solution)/shard_map/gradient/all_to_all | solution.py:60
  118.8 89.8 %all-gather.5.cloned.1.call-start = ((), (), s32[]{:S(2)}) async-start(), calls=%async_computation.6 | async-start | bytes 1966080 | tf_op jit(solution)/shard_map/gather_weights/all_gather | solution.py:32
  169.9 35.5 %copy-start.5 = (bf16[1024,2048]{1,0:T(8,128)(2,1)S(1)}, bf16[1024,2048]{1,0:T(8,128)(2,1)}, u32[]{:S(2)}) copy-start(bf16[1024,2048]{1,0:T(8,128)(2,1)} %all-gather.3.cloned.1.call-done) | copy-start | bytes 12582916
Sparse Core Ops, SparseCore 0:
  10.4 67.1 all-gather.2
  169.7 35.7 all-gather.4

commit v2 on v1

--- a/solution.py
+++ b/solution.py
@@ -29,7 +29,7 @@
         pair = spread(pair, ("yh", "yl"), n_y)
         pair = pair.transpose(2, 1, 0, 3, 4).reshape(2, n_zh * n_y * rows, width)
         last = spread(pair[0], "x", n_x)
-        first = lax.all_gather(pair[1], "x", axis=0, tiled=False)
+        full_grads, last = lax.optimization_barrier((full_grads, last))
 
     def in_order(w):
         return w.reshape(n_x, n_zh, n_y * rows, width).transpose(1, 0, 2, 3).reshape(units, width)
@@ -56,7 +56,9 @@
         parts = lax.all_to_all(
             grad_local.reshape(n_x * n_yl, units // (n_x * n_yl), width), ("x", "yl"), 0, 0
         )
+        parts, rest = lax.optimization_barrier((parts, pair[1]))
         part = jnp.sum(parts.astype(F32), axis=0).astype(BF)
+        first = lax.all_gather(rest, "x", axis=0, tiled=False)
         parts = lax.all_to_all(part.reshape(n_zh * n_yh, rows, width), ("zh", "yh"), 0, 0)
         gradient = jnp.sum(parts.astype(F32), axis=0)
 

time: 219 us -> 153 us (0.70); the launches traced: 218 us -> 150 us
  waiting for transfers between devices: 83.2 us -> 40.4 us
  blocking collectives: 90.2 us -> 50.4 us
  starting transfers between devices: 12.6 us -> 19.7 us
  matrix products: 8.86 us -> 11.8 us
  local copies, waits for them, and re-layouts: 6.03 us -> 8.28 us
    all_gather x1, waiting for transfers between devices: 68.2 us -> 0.01 us  [per_device(): full_grads = lax.all_gather(out_grad, ('zl', 'c'), axis=0, tiled=True)]
    all_to_all x0 -> x2, waiting for transfers between devices: none -> 28.8 us  [the longest x1 14.6 us: spread(): lax.all_to_all(jnp.broadcast_to(block[None], (size,) + block.shape), axes...]
    all_to_all x1 -> x0, blocking collectives: 22.1 us -> none  [per_device(): lax.all_to_all(grad_local.reshape(n_x * n_yl, units // (n_x * n_yl), widt...]
    all_to_all x3 -> x2, blocking collectives: 68.1 us -> 50.4 us  [spread(): lax.all_to_all(jnp.broadcast_to(block[None], (size,) + block.shape), axes...]
    all_to_all x0 -> x2, starting transfers between devices: none -> 11 us  [the longest x1 6.28 us: per_device(): lax.all_to_all(grad_local.reshape(n_x * n_yl, units // (n_x * n_yl), widt...]
    all_to_all x1, waiting for transfers between devices: 14.3 us -> 8.91 us  [per_device(): lax.all_to_all(part.reshape(n_zh * n_yh, rows, width), ('zh', 'yh'), 0, 0)]
    all_to_all x1, starting transfers between devices: 12.5 us -> 8.57 us  [per_device(): lax.all_to_all(part.reshape(n_zh * n_yh, rows, width), ('zh', 'yh'), 0, 0)]
    dot_general x1, matrix products: 3.26 us -> 6.2 us  [per_device(): lax.dot_general(scaled, in_order(last), (((1,), (1,)), ((), ())), preferr...]
  transfers between devices with their start and end apart: 3 -> 5, of which waited for: 2 -> 4; matrix products, arithmetic and copies ran while one was open for 2% -> 11% of each run, Pallas kernels for 0% -> 0%
where the time goes in v2:
time: 153 us; the launch traced here: 150 us
  blocking collectives  50.4 us (33%)
  waiting for transfers between devices  40.4 us (26%)
  starting transfers between devices  19.7 us (13%)
  between operations  14.9 us (10%)
  matrix products  11.8 us (8%)
  local copies, waits for them, and re-layouts  8.28 us (5%)
  other arithmetic  4.51 us (3%)
    all_to_all x2, blocking collectives, spread(): lax.all_to_all(jnp.broadcast_to(block[None], (size,) + block.shape), axes...  50.4 us
    all_to_all x1, waiting for transfers between devices, spread(): lax.all_to_all(jnp.broadcast_to(block[None], (size,) + block.shape), axes...  14.6 us
    all_to_all x1, waiting for transfers between devices, per_device(): lax.all_to_all(grad_local.reshape(n_x * n_yl, units // (n_x * n_yl), widt...  14.2 us
    all_to_all x1, waiting for transfers between devices, per_device(): lax.all_to_all(part.reshape(n_zh * n_yh, rows, width), ('zh', 'yh'), 0, 0)  8.91 us
    all_to_all x1, starting transfers between devices, per_device(): lax.all_to_all(part.reshape(n_zh * n_yh, rows, width), ('zh', 'yh'), 0, 0)  8.57 us
    all_to_all x1, starting transfers between devices, per_device(): lax.all_to_all(grad_local.reshape(n_x * n_yl, units // (n_x * n_yl), widt...  6.28 us
    dot_general x1, matrix products, per_device(): lax.dot_general(scaled, in_order(last), (((1,), (1,)), ((), ())), preferr...  6.2 us
    dot_general x1, matrix products, per_device(): lax.dot_general(ordered, scaled, (((0,), (0,)), ((), ())), preferred_elem...  5.6 us
  transfers between devices with their start and end apart: 5, of which 4 were waited for; matrix products, arithmetic and copies ran while one was open for 11% of the time, Pallas kernels for 0%

profile of v2, /device:TPU:6, one launch (start us, length us, event | category | flops | bytes accessed | tf_op | source)
XLA Modules:
  0.0 150.0 jit_solution(1268192546418127073)
XLA Ops:
  7.2 0.7 all-gather.4.cloned.1.call-update
  7.9 0.8 convert_bitcast_fusion
  8.7 0.7 pad_maximum_fusion
  9.5 21.8 %all_to_all.25 = bf16[3,2,4,2048]{3,2,1,0:T(4,128)(2,1)S(1)} all-to-all(bf16[3,2,4,2048]{3,2,1,0:T(4,128)(2,1)S(1)} %broadcast_in_dim.8), channel_id=1, replica_groups=mesh['zh'=3,'x'=4,'yh'=4,'yl'=2,'zl'=4,'c'=2] {'zh'}, dimensions={0} | all-to-all | bytes 196608 | tf_op jit(solution)/shard_map/gather_weights/all_to_all | solution.py:13
  31.3 0.4 broadcast_in_dim.9
  31.7 28.6 %all_to_all.26 = bf16[8,3,2,4,2048]{4,3,1,2,0:T(4,128)(2,1)S(1)} all-to-all(bf16[8,3,2,4,2048]{4,3,1,2,0:T(4,128)(2,1)S(1)} %broadcast_in_dim.9), channel_id=1, replica_groups=mesh['zh'=3,'x'=4,'yh'=4,'yl'=2,'zl'=4,'c'=2] {'yh','yl'}, dimensions={0} | all-to-all | bytes 1572864 | tf_op jit(solution)/shard_map/gather_weights/all_to_all | solution.py:13
  60.3 0.4 fusion.7
  61.0 1.3 broadcast_in_dim.11
  62.3 4.8 %all-to-all-start.2 = ((bf16[4,96,2048]{2,1,0:T(8,128)(2,1)}), bf16[4,96,2048]{2,1,0:T(8,128)(2,1)S(1)}, u32[]{:S(2)}, u32[]{:S(2)}) async-start(bf16[4,96,2048]{2,1,0:T(8,128)(2,1)} %broadcast_in_dim.11), calls=%async_computation.2 | async-start | bytes 3145728 | tf_op jit(solution)/shard_map/gather_weights/all_to_all | solution.py:13
  67.2 0.5 convert_reduce_fusion
  67.8 14.6 %all-to-all-done.2 = bf16[4,96,2048]{2,1,0:T(8,128)(2,1)S(1)} async-done(((bf16[4,96,2048]{2,1,0:T(8,128)(2,1)}), bf16[4,96,2048]{2,1,0:T(8,128)(2,1)S(1)}, u32[]{:S(2)}, u32[]{:S(2)}) %all-to-all-start.2) | async-done | bytes 1572896 | tf_op jit(solution)/shard_map/gather_weights/all_to_all | solution.py:13
  82.4 5.6 %convolution_convert_fusion = bf16[384,2048]{1,0:T(8,128)(2,1)} fusion(bf16[1024,2048]{1,0:T(8,128)(2,1)} %all-gather.4.cloned.1.call-done, f32[1024]{0:T(1024)S(1)} %broadcast_divide_fusion, bf16[1024,384]{1,0:T(8,128)(2,1)S(1)} %copy-done, s32[384]{0:T(512)S(1)} %reshape.141), kind=kOutput, calls=%fused_computation.2 | convolution fusion | flops 1920368640 | bytes 6559232 | tf_op jit(solution)/shard_map/gradient/dot_general | solution.py:53
  88.0 6.3 %all-to-all-start.3 = ((bf16[8,48,2048]{2,1,0:T(8,128)(2,1)}), bf16[8,48,2048]{2,1,0:T(8,128)(2,1)}, u32[]{:S(2)}, u32[]{:S(2)}) async-start(bf16[8,48,2048]{2,1,0:T(8,128)(2,1)} %bitcast.20), calls=%async_computation.3 | async-start | bytes 3145728 | tf_op jit(solution)/shard_map/gradient/all_to_all | solution.py:56
  94.5 0.8 squeeze.4
  95.3 14.2 %all-to-all-done.3 = bf16[8,48,2048]{2,1,0:T(8,128)(2,1)} async-done(((bf16[8,48,2048]{2,1,0:T(8,128)(2,1)}), bf16[8,48,2048]{2,1,0:T(8,128)(2,1)}, u32[]{:S(2)}, u32[]{:S(2)}) %all-to-all-start.3) | async-done | bytes 1572896 | tf_op jit(solution)/shard_map/gradient/all_to_all | solution.py:56
  110.2 1.2 copy.23
  111.5 1.7 %reduce_sum.31 = bf16[48,2048]{1,0:T(8,128)(2,1)S(1)} reduce(bf16[8,48,2048]{2,1,0:T(8,128)(2,1)} %all-to-all-done.3, bf16[]{:T(256)} %constant.27.clone.1), dimensions={0}, to_apply=%region_1.0 | reduce | flops 688128 | bytes 1769474 | tf_op jit(solution)/shard_map/gradient/reduce_sum | solution.py:60
  113.1 0.8 reshape.137
  113.9 8.6 %all-to-all-start.4 = ((bf16[12,4,2048]{2,1,0:T(4,128)(2,1)}), bf16[12,4,2048]{2,1,0:T(4,128)(2,1)S(1)}, u32[]{:S(2)}, u32[]{:S(2)}) async-start(bf16[12,4,2048]{2,1,0:T(4,128)(2,1)} %reshape.137), calls=%async_computation.4 | async-start | bytes 393216 | tf_op jit(solution)/shard_map/gradient/all_to_all | solution.py:62
  122.5 6.2 %fusion.1 = bf16[1024,384]{1,0:T(8,128)(2,1)} fusion(bf16[384,2048]{1,0:T(8,128)(2,1)} %bitcast.21, bf16[1024,2048]{1,0:T(8,128)(2,1)} %all-gather.4.cloned.1.call-done, f32[1024]{0:T(1024)S(1)} %broadcast_divide_fusion), kind=kOutput, calls=%fused_computation.4 | convolution fusion | flops 1617297408 | bytes 6557696 | tf_op jit(solution)/shard_map/hidden_grad/dot_general | solution.py:66
  128.7 8.9 %all-to-all-done.4 = bf16[12,4,2048]{2,1,0:T(4,128)(2,1)S(1)} async-done(((bf16[12,4,2048]{2,1,0:T(4,128)(2,1)}), bf16[12,4,2048]{2,1,0:T(4,128)(2,1)S(1)}, u32[]{:S(2)}, u32[]{:S(2)}) %all-to-all-start.4) | async-done | bytes 196640 | tf_op jit(solution)/shard_map/gradient/all_to_all | solution.py:62
  137.7 0.7 multiply_subtract_fusion
  138.4 2.0 %all-gather.6.cloned.1.call-done = bf16[384,2048]{1,0:T(8,128)(2,1)} async-done(((bf16[96,2048]{1,0:T(8,128)(2,1)}), bf16[384,2048]{1,0:T(8,128)(2,1)}) %all-gather.6.cloned.1.call-update) | async-done | bytes 1572880 | tf_op jit(solution)/shard_map/gradient/all_gather | solution.py:61
  140.4 2.7 %copy.25 = bf16[3,4,32,2048]{3,2,1,0:T(8,128)(2,1)} copy(bf16[3,4,32,2048]{3,2,0,1:T(8,128)(2,1)} %bitcast.18) | data formatting | bytes 3145728 | tf_op jit(solution)/shard_map/transpose | solution.py:35
  (23 shorter events, 0.8 us)
Async XLA Ops:
  7.2 75.2 %copy-start = (bf16[1024,384]{1,0:T(8,128)(2,1)S(1)}, bf16[1024,384]{1,0:T(8,128)(2,1)}, u32[]{:S(2)}) copy-start(bf16[1024,384]{1,0:T(8,128)(2,1)} %param.9) | copy-start | bytes 2359300
  7.2 75.2 %all-gather.4.cloned.1.call-start = ((), (), s32[]{:S(2)}) async-start(), calls=%async_computation.5 | async-start | bytes 4718592 | tf_op jit(solution)/shard_map/gather_grads/all_gather | solution.py:24
  60.3 6.9 %copy-start.4 = (s32[1,1024]{1,0:T(1,128)S(1)}, s32[1,1024]{1,0:T(1,128)}, u32[]{:S(2)}) copy-start(s32[1,1024]{1,0:T(1,128)} %param.10) | copy-start | bytes 12292
  62.3 20.1 %all-to-all-start.2 = ((bf16[4,96,2048]{2,1,0:T(8,128)(2,1)}), bf16[4,96,2048]{2,1,0:T(8,128)(2,1)S(1)}, u32[]{:S(2)}, u32[]{:S(2)}) async-start(bf16[4,96,2048]{2,1,0:T(8,128)(2,1)} %broadcast_in_dim.11), calls=%async_computation.2 | async-start | bytes 3145728 | tf_op jit(solution)/shard_map/gather_weights/all_to_all | solution.py:13
  88.0 21.5 %all-to-all-start.3 = ((bf16[8,48,2048]{2,1,0:T(8,128)(2,1)}), bf16[8,48,2048]{2,1,0:T(8,128)(2,1)}, u32[]{:S(2)}, u32[]{:S(2)}) async-start(bf16[8,48,2048]{2,1,0:T(8,128)(2,1)} %bitcast.20), calls=%async_computation.3 | async-start | bytes 3145728 | tf_op jit(solution)/shard_map/gradient/all_to_all | solution.py:56
  94.3 46.1 %all-gather.6.cloned.1.call-start = ((), (), s32[]{:S(2)}) async-start(), calls=%async_computation.6 | async-start | bytes 1966080 | tf_op jit(solution)/shard_map/gradient/all_gather | solution.py:61
  113.9 23.7 %all-to-all-start.4 = ((bf16[12,4,2048]{2,1,0:T(4,128)(2,1)}), bf16[12,4,2048]{2,1,0:T(4,128)(2,1)S(1)}, u32[]{:S(2)}, u32[]{:S(2)}) async-start(bf16[12,4,2048]{2,1,0:T(4,128)(2,1)} %reshape.137), calls=%async_computation.4 | async-start | bytes 393216 | tf_op jit(solution)/shard_map/gradient/all_to_all | solution.py:62
  122.5 15.2 %copy-start.1 = (f32[4,2048]{1,0:T(4,128)S(1)}, f32[4,2048]{1,0:T(4,128)}, u32[]{:S(2)}) copy-start(f32[4,2048]{1,0:T(4,128)} %param.11) | copy-start | bytes 98308
  122.5 15.2 %copy-start.2 = (f32[4,2048]{1,0:T(4,128)S(1)}, f32[4,2048]{1,0:T(4,128)}, u32[]{:S(2)}) copy-start(f32[4,2048]{1,0:T(4,128)} %param.13) | copy-start | bytes 98308
  122.5 15.2 %copy-start.3 = (f32[4,2048]{1,0:T(4,128)S(1)}, f32[4,2048]{1,0:T(4,128)}, u32[]{:S(2)}) copy-start(f32[4,2048]{1,0:T(4,128)} %param.12) | copy-start | bytes 98308
Sparse Core Ops, SparseCore 0:
  10.4 67.1 all-gather.3
  109.6 30.7 all-gather.5

commit v3 on v1

--- a/solution.py
+++ b/solution.py
@@ -1,12 +1,21 @@
 import jax
 import jax.numpy as jnp
 from jax import lax
+from jax.experimental import pallas as pl
+from jax.experimental.pallas import tpu as pltpu
 from jax.sharding import Mesh
 from jax.sharding import PartitionSpec as P
 
 DOCS = 8
 BF = jnp.bfloat16
 F32 = jnp.float32
+
+
+def sum_kernel(parts, out, total):
+    total[...] = jnp.sum(parts[...].astype(F32), axis=0)
+    rows = out.shape[1]
+    for i in range(out.shape[0]):
+        out[i] = total[i * rows:(i + 1) * rows, :].astype(BF)
 
 
 def spread(block, axes, size):
@@ -30,6 +39,7 @@
         pair = pair.transpose(2, 1, 0, 3, 4).reshape(2, n_zh * n_y * rows, width)
         last = spread(pair[0], "x", n_x)
         first = lax.all_gather(pair[1], "x", axis=0, tiled=False)
+        full_grads, last = lax.optimization_barrier((full_grads, last))
 
     def in_order(w):
         return w.reshape(n_x, n_zh, n_y * rows, width).transpose(1, 0, 2, 3).reshape(units, width)
@@ -42,12 +52,18 @@
         scaled = (full_grads.astype(F32) * weight[:, None]).astype(BF)
 
     with jax.named_scope("unit_order"):
-        place = jnp.arange(units, dtype=jnp.int32).reshape(n_zh, n_x, n_yh, n_yl, rows)
-        place = place.transpose(1, 3, 0, 2, 4).reshape(units)
-        pick = (jnp.arange(units, dtype=jnp.int32)[:, None] == place[None, :]).astype(BF)
+        at = jnp.arange(units, dtype=jnp.int32)
+        order = at.reshape(n_zh, n_x, n_yh, n_yl, rows).transpose(1, 3, 0, 2, 4).reshape(units)
+        pick = (at[:, None] == order[None, :]).astype(BF)
         ordered = lax.dot_general(
             hidden, pick, (((1,), (0,)), ((), ())), preferred_element_type=F32
         ).astype(BF)
+
+    with jax.named_scope("hidden_grad"):
+        hidden_grad = lax.dot_general(
+            scaled, in_order(last), (((1,), (1,)), ((), ())), preferred_element_type=F32
+        )
+        hidden_grad = hidden_grad.astype(BF)
 
     with jax.named_scope("gradient"):
         grad_local = lax.dot_general(
@@ -56,14 +72,19 @@
         parts = lax.all_to_all(
             grad_local.reshape(n_x * n_yl, units // (n_x * n_yl), width), ("x", "yl"), 0, 0
         )
-        part = jnp.sum(parts.astype(F32), axis=0).astype(BF)
-        parts = lax.all_to_all(part.reshape(n_zh * n_yh, rows, width), ("zh", "yh"), 0, 0)
+        parts, hidden_grad = lax.optimization_barrier((parts, hidden_grad))
+        vmem = pl.BlockSpec(memory_space=pltpu.VMEM)
+        part = pl.pallas_call(
+            sum_kernel,
+            out_shape=jax.ShapeDtypeStruct((n_zh * n_yh, rows, width), BF),
+            in_specs=[vmem],
+            out_specs=vmem,
+            scratch_shapes=[pltpu.VMEM((n_zh * n_yh * rows, width), F32)],
+            compiler_params=pltpu.CompilerParams(vmem_limit_bytes=16 << 20),
+        )(parts)
+        parts = lax.all_to_all(part, ("zh", "yh"), 0, 0)
+        parts, first = lax.optimization_barrier((parts, first))
         gradient = jnp.sum(parts.astype(F32), axis=0)
-
-    with jax.named_scope("hidden_grad"):
-        hidden_grad = lax.dot_general(
-            scaled, in_order(last), (((1,), (1,)), ((), ())), preferred_element_type=F32
-        )
 
     with jax.named_scope("adamw"):
         gradient = gradient / all_tokens
@@ -78,7 +99,7 @@
         )
         new_master = master - 0.00015 * update
     return (
-        hidden_grad.astype(BF),
+        hidden_grad,
         new_master,
         new_moment_one,
         new_moment_two,

time: 219 us -> 147 us (0.67)
  waiting for transfers between devices: 83.2 us -> 36.6 us
  blocking collectives: 90.2 us -> 50.4 us
  starting transfers between devices: 12.6 us -> 18.8 us
  matrix products: 8.86 us -> 11.6 us
    all_gather x1, waiting for transfers between devices: 68.2 us -> 0.01 us  [per_device(): full_grads = lax.all_gather(out_grad, ('zl', 'c'), axis=0, tiled=True)]
    all_to_all x1 -> x0, blocking collectives: 22.1 us -> none  [per_device(): lax.all_to_all(grad_local.reshape(n_x * n_yl, units // (n_x * n_yl), widt...]
    all_to_all x3 -> x2, blocking collectives: 68.1 us -> 50.4 us  [spread(): lax.all_to_all(jnp.broadcast_to(block[None], (size,) + block.shape), axes...]
    all_to_all x1 -> x3, waiting for transfers between devices: 14.3 us -> 29.5 us  [the longest x1 14.6 us: spread(): lax.all_to_all(jnp.broadcast_to(block[None], (size,) + block.shape), axes...]
    all_gather x1, waiting for transfers between devices: 0.01 us -> 6.43 us  [per_device(): first = lax.all_gather(pair[1], 'x', axis=0, tiled=False)]
    all_to_all x1 -> x3, starting transfers between devices: 12.5 us -> 18.7 us  [the longest x1 8.39 us: per_device(): parts = lax.all_to_all(part, ('zh', 'yh'), 0, 0)]
  transfers between devices with their start and end apart: 3 -> 5, of which waited for: 2 -> 4; matrix products, arithmetic and copies ran while one was open for 2% -> 9% of each run, Pallas kernels for 0% -> 1%
where the time goes in v3:
time: 147 us; the launch traced here: 145 us
  blocking collectives  50.4 us (34%)
  waiting for transfers between devices  36.6 us (25%)
  starting transfers between devices  18.8 us (13%)
  between operations  16.3 us (11%)
  matrix products  11.6 us (8%)
  local copies, waits for them, and re-layouts  7.69 us (5%)
  other arithmetic  2.86 us (2%)
    all_to_all x2, blocking collectives, spread(): lax.all_to_all(jnp.broadcast_to(block[None], (size,) + block.shape), axes...  50.4 us
    all_to_all x1, waiting for transfers between devices, spread(): lax.all_to_all(jnp.broadcast_to(block[None], (size,) + block.shape), axes...  14.6 us
    all_to_all x1, starting transfers between devices, per_device(): parts = lax.all_to_all(part, ('zh', 'yh'), 0, 0)  8.39 us
    all_to_all x1, waiting for transfers between devices, per_device(): parts = lax.all_to_all(part, ('zh', 'yh'), 0, 0)  7.74 us
    all_to_all x1, waiting for transfers between devices, per_device(): lax.all_to_all(grad_local.reshape(n_x * n_yl, units // (n_x * n_yl), widt...  7.09 us
    all_gather x1, waiting for transfers between devices, per_device(): first = lax.all_gather(pair[1], 'x', axis=0, tiled=False)  6.43 us
    dot_general x1, matrix products, per_device(): lax.dot_general(ordered, scaled, (((0,), (0,)), ((), ())), preferred_elem...  6.2 us
    all_to_all x1, starting transfers between devices, per_device(): lax.all_to_all(grad_local.reshape(n_x * n_yl, units // (n_x * n_yl), widt...  5.58 us
  transfers between devices with their start and end apart: 5, of which 4 were waited for; matrix products, arithmetic and copies ran while one was open for 9% of the time, Pallas kernels for 1%

profile of v3, /device:TPU:6, one launch (start us, length us, event | category | flops | bytes accessed | tf_op | source)
XLA Modules:
  0.0 145.3 jit_solution(15985376811322093829)
XLA Ops:
  8.1 0.7 all-gather.3.cloned.1.call-update
  8.7 0.8 convert_bitcast_fusion
  9.5 0.7 pad_maximum_fusion
  10.3 21.8 %all_to_all.25 = bf16[3,2,4,2048]{3,2,1,0:T(4,128)(2,1)S(1)} all-to-all(bf16[3,2,4,2048]{3,2,1,0:T(4,128)(2,1)S(1)} %broadcast_in_dim.8), channel_id=1, replica_groups=mesh['zh'=3,'x'=4,'yh'=4,'yl'=2,'zl'=4,'c'=2] {'zh'}, dimensions={0} | all-to-all | bytes 196608 | tf_op jit(solution)/shard_map/gather_weights/all_to_all | solution.py:22
  32.2 0.4 broadcast_in_dim.9
  32.5 28.6 %all_to_all.26 = bf16[8,3,2,4,2048]{4,3,1,2,0:T(4,128)(2,1)S(1)} all-to-all(bf16[8,3,2,4,2048]{4,3,1,2,0:T(4,128)(2,1)S(1)} %broadcast_in_dim.9), channel_id=1, replica_groups=mesh['zh'=3,'x'=4,'yh'=4,'yl'=2,'zl'=4,'c'=2] {'yh','yl'}, dimensions={0} | all-to-all | bytes 1572864 | tf_op jit(solution)/shard_map/gather_weights/all_to_all | solution.py:22
  61.2 0.3 fusion.7
  61.7 1.3 broadcast_in_dim.11
  63.0 4.8 %all-to-all-start.2 = ((bf16[4,96,2048]{2,1,0:T(8,128)(2,1)}), bf16[4,96,2048]{2,1,0:T(8,128)(2,1)S(1)}, u32[]{:S(2)}, u32[]{:S(2)}) async-start(bf16[4,96,2048]{2,1,0:T(8,128)(2,1)} %broadcast_in_dim.11), calls=%async_computation.2 | async-start | bytes 3145728 | tf_op jit(solution)/shard_map/gather_weights/all_to_all | solution.py:22
  68.0 0.5 convert_reduce_fusion
  68.5 14.6 %all-to-all-done.2 = bf16[4,96,2048]{2,1,0:T(8,128)(2,1)S(1)} async-done(((bf16[4,96,2048]{2,1,0:T(8,128)(2,1)}), bf16[4,96,2048]{2,1,0:T(8,128)(2,1)S(1)}, u32[]{:S(2)}, u32[]{:S(2)}) %all-to-all-start.2) | async-done | bytes 1572896 | tf_op jit(solution)/shard_map/gather_weights/all_to_all | solution.py:22
  83.1 6.2 %convolution_convert_fusion = bf16[384,2048]{1,0:T(8,128)(2,1)} fusion(bf16[1024,2048]{1,0:T(8,128)(2,1)} %all-gather.3.cloned.1.call-done, f32[1024]{0:T(1024)S(1)} %broadcast_divide_fusion, bf16[1024,384]{1,0:T(8,128)(2,1)S(1)} %copy-done, s32[384]{0:T(512)S(1)} %reshape.136), kind=kOutput, calls=%fused_computation.2 | convolution fusion | flops 1920368640 | bytes 6559232 | tf_op jit(solution)/shard_map/gradient/dot_general | solution.py:69
  89.3 5.6 %all-to-all-start.3 = ((bf16[8,48,2048]{2,1,0:T(8,128)(2,1)}), bf16[8,48,2048]{2,1,0:T(8,128)(2,1)S(1)}, u32[]{:S(2)}, u32[]{:S(2)}) async-start(bf16[8,48,2048]{2,1,0:T(8,128)(2,1)} %bitcast.19), calls=%async_computation.3 | async-start | bytes 3145728 | tf_op jit(solution)/shard_map/gradient/all_to_all | solution.py:72
  94.9 0.2 copy.24
  95.1 0.8 slice.12
  96.0 1.5 %copy.23 = bf16[3,4,32,2048]{3,2,1,0:T(8,128)(2,1)S(1)} copy(bf16[3,4,32,2048]{3,2,0,1:T(8,128)(2,1)} %bitcast.16) | data formatting | bytes 3145728 | tf_op jit(solution)/shard_map/hidden_grad/transpose | solution.py:45
  97.5 5.4 %fusion.1 = bf16[1024,384]{1,0:T(8,128)(2,1)} fusion(bf16[384,2048]{1,0:T(8,128)(2,1)S(1)} %bitcast.21, bf16[1024,2048]{1,0:T(8,128)(2,1)} %all-gather.3.cloned.1.call-done, f32[1024]{0:T(1024)S(1)} %broadcast_divide_fusion), kind=kOutput, calls=%fused_computation.4 | convolution fusion | flops 1617297408 | bytes 6557696 | tf_op jit(solution)/shard_map/hidden_grad/dot_general | solution.py:63
  102.9 7.1 %all-to-all-done.3.parts = bf16[8,48,2048]{2,1,0:T(8,128)(2,1)S(1)} async-done(((bf16[8,48,2048]{2,1,0:T(8,128)(2,1)}), bf16[8,48,2048]{2,1,0:T(8,128)(2,1)S(1)}, u32[]{:S(2)}, u32[]{:S(2)}) %all-to-all-start.3) | async-done | bytes 1572896 | tf_op jit(solution)/shard_map/gradient/all_to_all | solution.py:72
  110.0 1.0 gradient.1
  111.0 8.4 %all-to-all-start.4 = ((bf16[12,4,2048]{2,1,0:T(4,128)(2,1)}), bf16[12,4,2048]{2,1,0:T(4,128)(2,1)S(1)}, u32[]{:S(2)}, u32[]{:S(2)}) async-start(bf16[12,4,2048]{2,1,0:T(4,128)(2,1)} %gradient.1), calls=%async_computation.4 | async-start | bytes 393216 | tf_op jit(solution)/shard_map/gradient/all_to_all | solution.py:85
  120.1 6.4 %all-gather.5.cloned.1.call-done = bf16[4,96,2048]{2,1,0:T(8,128)(2,1)} async-done(((bf16[1,96,2048]{2,1,0:T(8,128)(2,1)}), bf16[4,96,2048]{2,1,0:T(8,128)(2,1)}) %all-gather.5.cloned.1.call-update) | async-done | bytes 1572880 | tf_op jit(solution)/shard_map/gather_weights/all_gather | solution.py:41
  126.6 7.7 %all-to-all-done.4 = bf16[12,4,2048]{2,1,0:T(4,128)(2,1)S(1)} async-done(((bf16[12,4,2048]{2,1,0:T(4,128)(2,1)}), bf16[12,4,2048]{2,1,0:T(4,128)(2,1)S(1)}, u32[]{:S(2)}, u32[]{:S(2)}) %all-to-all-start.4) | async-done | bytes 196640 | tf_op jit(solution)/shard_map/gradient/all_to_all | solution.py:85
  134.4 2.7 %copy.25 = bf16[3,4,32,2048]{3,2,1,0:T(8,128)(2,1)} copy(bf16[3,4,32,2048]{3,2,0,1:T(8,128)(2,1)} %bitcast.18) | data formatting | bytes 3145728 | tf_op jit(solution)/shard_map/transpose | solution.py:45
  137.1 0.7 multiply_subtract_fusion
  (24 shorter events, 0.6 us)
Async XLA Ops:
  8.0 75.1 %copy-start = (bf16[1024,384]{1,0:T(8,128)(2,1)S(1)}, bf16[1024,384]{1,0:T(8,128)(2,1)}, u32[]{:S(2)}) copy-start(bf16[1024,384]{1,0:T(8,128)(2,1)} %param.9) | copy-start | bytes 2359300
  8.0 75.1 %all-gather.3.cloned.1.call-start = ((), (), s32[]{:S(2)}) async-start(), calls=%async_computation.5 | async-start | bytes 4718592 | tf_op jit(solution)/shard_map/gather_grads/all_gather | solution.py:33
  61.2 6.8 %copy-start.5 = (s32[1,1024]{1,0:T(1,128)S(1)}, s32[1,1024]{1,0:T(1,128)}, u32[]{:S(2)}) copy-start(s32[1,1024]{1,0:T(1,128)} %param.10) | copy-start | bytes 12292
  63.0 20.1 %all-to-all-start.2 = ((bf16[4,96,2048]{2,1,0:T(8,128)(2,1)}), bf16[4,96,2048]{2,1,0:T(8,128)(2,1)S(1)}, u32[]{:S(2)}, u32[]{:S(2)}) async-start(bf16[4,96,2048]{2,1,0:T(8,128)(2,1)} %broadcast_in_dim.11), calls=%async_computation.2 | async-start | bytes 3145728 | tf_op jit(solution)/shard_map/gather_weights/all_to_all | solution.py:22
  83.1 6.2 %copy-start.1 = (bf16[4,96,2048]{2,1,0:T(8,128)(2,1)}, bf16[4,96,2048]{2,1,0:T(8,128)(2,1)S(1)}, u32[]{:S(2)}) copy-start(bf16[4,96,2048]{2,1,0:T(8,128)(2,1)S(1)} %all-to-all-done.2) | copy-start | bytes 4718596
  89.3 20.7 %all-to-all-start.3 = ((bf16[8,48,2048]{2,1,0:T(8,128)(2,1)}), bf16[8,48,2048]{2,1,0:T(8,128)(2,1)S(1)}, u32[]{:S(2)}, u32[]{:S(2)}) async-start(bf16[8,48,2048]{2,1,0:T(8,128)(2,1)} %bitcast.19), calls=%async_computation.3 | async-start | bytes 3145728 | tf_op jit(solution)/shard_map/gradient/all_to_all | solution.py:72
  94.9 31.6 %all-gather.5.cloned.1.call-start = ((), (), s32[]{:S(2)}) async-start(), calls=%async_computation.6 | async-start | bytes 1966080 | tf_op jit(solution)/shard_map/gather_weights/all_gather | solution.py:41
  102.9 34.2 %copy-start.2 = (f32[4,2048]{1,0:T(4,128)S(1)}, f32[4,2048]{1,0:T(4,128)}, u32[]{:S(2)}) copy-start(f32[4,2048]{1,0:T(4,128)} %param.11) | copy-start | bytes 98308
  102.9 34.2 %copy-start.3 = (f32[4,2048]{1,0:T(4,128)S(1)}, f32[4,2048]{1,0:T(4,128)}, u32[]{:S(2)}) copy-start(f32[4,2048]{1,0:T(4,128)} %param.13) | copy-start | bytes 98308
  102.9 34.2 %copy-start.4 = (f32[4,2048]{1,0:T(4,128)S(1)}, f32[4,2048]{1,0:T(4,128)}, u32[]{:S(2)}) copy-start(f32[4,2048]{1,0:T(4,128)} %param.12) | copy-start | bytes 98308
  111.0 23.3 %all-to-all-start.4 = ((bf16[12,4,2048]{2,1,0:T(4,128)(2,1)}), bf16[12,4,2048]{2,1,0:T(4,128)(2,1)S(1)}, u32[]{:S(2)}, u32[]{:S(2)}) async-start(bf16[12,4,2048]{2,1,0:T(4,128)(2,1)} %gradient.1), calls=%async_computation.4 | async-start | bytes 393216 | tf_op jit(solution)/shard_map/gradient/all_to_all | solution.py:85
Sparse Core Ops, SparseCore 0:
  11.2 67.1 all-gather.2
Sparse Core Ops, SparseCore 1:
  97.8 28.7 all-gather.4

commit v4 on v3

--- a/solution.py
+++ b/solution.py
@@ -39,10 +39,18 @@
         pair = pair.transpose(2, 1, 0, 3, 4).reshape(2, n_zh * n_y * rows, width)
         last = spread(pair[0], "x", n_x)
         first = lax.all_gather(pair[1], "x", axis=0, tiled=False)
-        full_grads, last = lax.optimization_barrier((full_grads, last))
-
     def in_order(w):
         return w.reshape(n_x, n_zh, n_y * rows, width).transpose(1, 0, 2, 3).reshape(units, width)
+
+    with jax.named_scope("unit_order"):
+        at = jnp.arange(units, dtype=jnp.int32)
+        order = at.reshape(n_zh, n_x, n_yh, n_yl, rows).transpose(1, 3, 0, 2, 4).reshape(units)
+        pick = (order[:, None] == at[None, :]).astype(BF)
+        hidden_t = lax.dot_general(
+            pick, hidden, (((1,), (1,)), ((), ())), preferred_element_type=F32
+        ).astype(BF)
+
+    full_grads, last, hidden_t = lax.optimization_barrier((full_grads, last, hidden_t))
 
     with jax.named_scope("weights_of_tokens"):
         seg_row = segments[0]
@@ -50,14 +58,6 @@
         doc_len = jnp.sum(same_doc, axis=1)
         weight = tok_dev / DOCS / doc_len
         scaled = (full_grads.astype(F32) * weight[:, None]).astype(BF)
-
-    with jax.named_scope("unit_order"):
-        at = jnp.arange(units, dtype=jnp.int32)
-        order = at.reshape(n_zh, n_x, n_yh, n_yl, rows).transpose(1, 3, 0, 2, 4).reshape(units)
-        pick = (at[:, None] == order[None, :]).astype(BF)
-        ordered = lax.dot_general(
-            hidden, pick, (((1,), (0,)), ((), ())), preferred_element_type=F32
-        ).astype(BF)
 
     with jax.named_scope("hidden_grad"):
         hidden_grad = lax.dot_general(
@@ -67,7 +67,7 @@
 
     with jax.named_scope("gradient"):
         grad_local = lax.dot_general(
-            ordered, scaled, (((0,), (0,)), ((), ())), preferred_element_type=F32
+            hidden_t, scaled, (((1,), (0,)), ((), ())), preferred_element_type=F32
         ).astype(BF)
         parts = lax.all_to_all(
             grad_local.reshape(n_x * n_yl, units // (n_x * n_yl), width), ("x", "yl"), 0, 0
@@ -83,7 +83,7 @@
             compiler_params=pltpu.CompilerParams(vmem_limit_bytes=16 << 20),
         )(parts)
         parts = lax.all_to_all(part, ("zh", "yh"), 0, 0)
-        parts, first = lax.optimization_barrier((parts, first))
+        parts, first = lax.optimization_barrier((parts, in_order(first)))
         gradient = jnp.sum(parts.astype(F32), axis=0)
 
     with jax.named_scope("adamw"):
@@ -104,7 +104,7 @@
         new_moment_one,
         new_moment_two,
         update,
-        in_order(first),
+        first,
     )
 
 

time: 147 us -> 144 us (0.980)
  waiting for transfers between devices: 36.6 us -> 33.2 us
    all_to_all x1, waiting for transfers between devices: 7.74 us -> 4.9 us  [per_device(): parts = lax.all_to_all(part, ('zh', 'yh'), 0, 0)]
    dot_general x1 -> x2, matrix products: 6.2 us -> 6.43 us  [the longest x1 5.81 us: per_device(): lax.dot_general(hidden_t, scaled, (((1,), (0,)), ((), ())), preferred_ele...]
  transfers between devices with their start and end apart: 5 -> 5, of which waited for: 4 -> 4; matrix products, arithmetic and copies ran while one was open for 9% -> 11% of each run, Pallas kernels for 1% -> 1%
where the time goes in v4:
time: 144 us; the launch traced here: 142 us
  blocking collectives  50.4 us (35%)
  waiting for transfers between devices  33.2 us (23%)
  starting transfers between devices  18.7 us (13%)
  between operations  16.3 us (11%)
  matrix products  11.9 us (8%)
  local copies, waits for them, and re-layouts  7.78 us (5%)
  other arithmetic  2.86 us (2%)
    all_to_all x2, blocking collectives, spread(): lax.all_to_all(jnp.broadcast_to(block[None], (size,) + block.shape), axes...  50.4 us
    all_to_all x1, waiting for transfers between devices, spread(): lax.all_to_all(jnp.broadcast_to(block[None], (size,) + block.shape), axes...  14 us
    all_to_all x1, starting transfers between devices, per_device(): parts = lax.all_to_all(part, ('zh', 'yh'), 0, 0)  8.3 us
    all_to_all x1, waiting for transfers between devices, per_device(): lax.all_to_all(grad_local.reshape(n_x * n_yl, units // (n_x * n_yl), widt...  7.09 us
    all_gather x1, waiting for transfers between devices, per_device(): first = lax.all_gather(pair[1], 'x', axis=0, tiled=False)  6.5 us
    dot_general x1, matrix products, per_device(): lax.dot_general(hidden_t, scaled, (((1,), (0,)), ((), ())), preferred_ele...  5.81 us
    all_to_all x1, starting transfers between devices, per_device(): lax.all_to_all(grad_local.reshape(n_x * n_yl, units // (n_x * n_yl), widt...  5.59 us
    dot_general x1, matrix products, per_device(): lax.dot_general(scaled, in_order(last), (((1,), (1,)), ((), ())), preferr...  5.44 us
  transfers between devices with their start and end apart: 5, of which 4 were waited for; matrix products, arithmetic and copies ran while one was open for 11% of the time, Pallas kernels for 1%

profile of v4, /device:TPU:6, one launch (start us, length us, event | category | flops | bytes accessed | tf_op | source)
XLA Modules:
  0.0 142.2 jit_solution(2607312243600173189)
XLA Ops:
  8.1 0.7 all-gather.3.cloned.1.call-update
  8.7 0.8 convert_bitcast_fusion
  9.5 0.7 pad_maximum_fusion
  10.3 21.8 %all_to_all.25 = bf16[3,2,4,2048]{3,2,1,0:T(4,128)(2,1)S(1)} all-to-all(bf16[3,2,4,2048]{3,2,1,0:T(4,128)(2,1)S(1)} %broadcast_in_dim.8), channel_id=1, replica_groups=mesh['zh'=3,'x'=4,'yh'=4,'yl'=2,'zl'=4,'c'=2] {'zh'}, dimensions={0} | all-to-all | bytes 196608 | tf_op jit(solution)/shard_map/gather_weights/all_to_all | solution.py:22
  32.2 0.4 broadcast_in_dim.9
  32.5 28.6 %all_to_all.26 = bf16[8,3,2,4,2048]{4,3,1,2,0:T(4,128)(2,1)S(1)} all-to-all(bf16[8,3,2,4,2048]{4,3,1,2,0:T(4,128)(2,1)S(1)} %broadcast_in_dim.9), channel_id=1, replica_groups=mesh['zh'=3,'x'=4,'yh'=4,'yl'=2,'zl'=4,'c'=2] {'yh','yl'}, dimensions={0} | all-to-all | bytes 1572864 | tf_op jit(solution)/shard_map/gather_weights/all_to_all | solution.py:22
  61.2 0.4 fusion.3
  61.8 1.3 broadcast_in_dim.11
  63.1 4.8 %all-to-all-start.2 = ((bf16[4,96,2048]{2,1,0:T(8,128)(2,1)}), bf16[4,96,2048]{2,1,0:T(8,128)(2,1)S(1)}, u32[]{:S(2)}, u32[]{:S(2)}) async-start(bf16[4,96,2048]{2,1,0:T(8,128)(2,1)} %broadcast_in_dim.11), calls=%async_computation.2 | async-start | bytes 3145728 | tf_op jit(solution)/shard_map/gather_weights/all_to_all | solution.py:22
  68.0 0.5 convert_reduce_fusion
  68.6 0.6 convolution_convert_fusion.1
  69.2 14.0 %all-to-all-done.2 = bf16[4,96,2048]{2,1,0:T(8,128)(2,1)S(1)} async-done(((bf16[4,96,2048]{2,1,0:T(8,128)(2,1)}), bf16[4,96,2048]{2,1,0:T(8,128)(2,1)S(1)}, u32[]{:S(2)}, u32[]{:S(2)}) %all-to-all-start.2) | async-done | bytes 1572896 | tf_op jit(solution)/shard_map/gather_weights/all_to_all | solution.py:22
  83.2 5.8 %convolution_convert_fusion = bf16[384,2048]{1,0:T(8,128)(2,1)} fusion(bf16[384,1024]{1,0:T(8,128)(2,1)S(1)} %convolution_convert_fusion.1, bf16[1024,2048]{1,0:T(8,128)(2,1)} %all-gather.3.cloned.1.call-done, f32[1024]{0:T(1024)S(1)} %broadcast_divide_fusion), kind=kOutput, calls=%fused_computation.2 | convolution fusion | flops 1617690624 | bytes 6557696 | tf_op jit(solution)/shard_map/gradient/dot_general | solution.py:69
  89.0 5.6 %all-to-all-start.3 = ((bf16[8,48,2048]{2,1,0:T(8,128)(2,1)}), bf16[8,48,2048]{2,1,0:T(8,128)(2,1)S(1)}, u32[]{:S(2)}, u32[]{:S(2)}) async-start(bf16[8,48,2048]{2,1,0:T(8,128)(2,1)} %bitcast.20), calls=%async_computation.3 | async-start | bytes 3145728 | tf_op jit(solution)/shard_map/gradient/all_to_all | solution.py:72
  94.8 0.8 slice.12
  95.7 1.5 %copy.23 = bf16[3,4,32,2048]{3,2,1,0:T(8,128)(2,1)S(1)} copy(bf16[3,4,32,2048]{3,2,0,1:T(8,128)(2,1)} %bitcast.17) | data formatting | bytes 3145728 | tf_op jit(solution)/shard_map/hidden_grad/transpose | solution.py:43
  97.2 5.4 %fusion.1 = bf16[1024,384]{1,0:T(8,128)(2,1)} fusion(bf16[384,2048]{1,0:T(8,128)(2,1)S(1)} %bitcast.22, bf16[1024,2048]{1,0:T(8,128)(2,1)} %all-gather.3.cloned.1.call-done, f32[1024]{0:T(1024)S(1)} %broadcast_divide_fusion), kind=kOutput, calls=%fused_computation.4 | convolution fusion | flops 1617297408 | bytes 6557696 | tf_op jit(solution)/shard_map/hidden_grad/dot_general | solution.py:63
  102.6 7.1 %all-to-all-done.3.parts = bf16[8,48,2048]{2,1,0:T(8,128)(2,1)S(1)} async-done(((bf16[8,48,2048]{2,1,0:T(8,128)(2,1)}), bf16[8,48,2048]{2,1,0:T(8,128)(2,1)S(1)}, u32[]{:S(2)}, u32[]{:S(2)}) %all-to-all-start.3) | async-done | bytes 1572896 | tf_op jit(solution)/shard_map/gradient/all_to_all | solution.py:72
  109.7 1.0 gradient.1
  110.7 8.3 %all-to-all-start.4 = ((bf16[12,4,2048]{2,1,0:T(4,128)(2,1)}), bf16[12,4,2048]{2,1,0:T(4,128)(2,1)S(1)}, u32[]{:S(2)}, u32[]{:S(2)}) async-start(bf16[12,4,2048]{2,1,0:T(4,128)(2,1)} %gradient.1), calls=%async_computation.4 | async-start | bytes 393216 | tf_op jit(solution)/shard_map/gradient/all_to_all | solution.py:85
  119.8 6.5 %all-gather.5.cloned.1.call-done = bf16[4,96,2048]{2,1,0:T(8,128)(2,1)} async-done(((bf16[1,96,2048]{2,1,0:T(8,128)(2,1)}), bf16[4,96,2048]{2,1,0:T(8,128)(2,1)}) %all-gather.5.cloned.1.call-update) | async-done | bytes 1572880 | tf_op jit(solution)/shard_map/gather_weights/all_gather | solution.py:41
  126.3 2.7 %copy.25 = bf16[3,4,32,2048]{3,2,1,0:T(8,128)(2,1)} copy(bf16[3,4,32,2048]{3,2,0,1:T(8,128)(2,1)} %bitcast.19) | data formatting | bytes 3145728 | tf_op jit(solution)/shard_map/gradient/transpose | solution.py:43
  129.0 4.9 %all-to-all-done.4 = bf16[12,4,2048]{2,1,0:T(4,128)(2,1)S(1)} async-done(((bf16[12,4,2048]{2,1,0:T(4,128)(2,1)}), bf16[12,4,2048]{2,1,0:T(4,128)(2,1)S(1)}, u32[]{:S(2)}, u32[]{:S(2)}) %all-to-all-start.4) | async-done | bytes 196640 | tf_op jit(solution)/shard_map/gradient/all_to_all | solution.py:85
  134.0 0.7 multiply_subtract_fusion
  (25 shorter events, 0.8 us)
Async XLA Ops:
  8.0 60.6 %copy-start = (bf16[1024,384]{1,0:T(8,128)(2,1)S(1)}, bf16[1024,384]{1,0:T(8,128)(2,1)}, u32[]{:S(2)}) copy-start(bf16[1024,384]{1,0:T(8,128)(2,1)} %param.9) | copy-start | bytes 2359300
  8.0 75.2 %all-gather.3.cloned.1.call-start = ((), (), s32[]{:S(2)}) async-start(), calls=%async_computation.5 | async-start | bytes 4718592 | tf_op jit(solution)/shard_map/gather_grads/all_gather | solution.py:33
  61.2 6.9 %copy-start.5 = (s32[1,1024]{1,0:T(1,128)S(1)}, s32[1,1024]{1,0:T(1,128)}, u32[]{:S(2)}) copy-start(s32[1,1024]{1,0:T(1,128)} %param.10) | copy-start | bytes 12292
  63.1 20.1 %all-to-all-start.2 = ((bf16[4,96,2048]{2,1,0:T(8,128)(2,1)}), bf16[4,96,2048]{2,1,0:T(8,128)(2,1)S(1)}, u32[]{:S(2)}, u32[]{:S(2)}) async-start(bf16[4,96,2048]{2,1,0:T(8,128)(2,1)} %broadcast_in_dim.11), calls=%async_computation.2 | async-start | bytes 3145728 | tf_op jit(solution)/shard_map/gather_weights/all_to_all | solution.py:22
  83.2 5.8 %copy-start.1 = (bf16[4,96,2048]{2,1,0:T(8,128)(2,1)}, bf16[4,96,2048]{2,1,0:T(8,128)(2,1)S(1)}, u32[]{:S(2)}) copy-start(bf16[4,96,2048]{2,1,0:T(8,128)(2,1)S(1)} %all-to-all-done.2) | copy-start | bytes 4718596
  89.0 20.7 %all-to-all-start.3 = ((bf16[8,48,2048]{2,1,0:T(8,128)(2,1)}), bf16[8,48,2048]{2,1,0:T(8,128)(2,1)S(1)}, u32[]{:S(2)}, u32[]{:S(2)}) async-start(bf16[8,48,2048]{2,1,0:T(8,128)(2,1)} %bitcast.20), calls=%async_computation.3 | async-start | bytes 3145728 | tf_op jit(solution)/shard_map/gradient/all_to_all | solution.py:72
  94.6 31.6 %all-gather.5.cloned.1.call-start = ((), (), s32[]{:S(2)}) async-start(), calls=%async_computation.6 | async-start | bytes 1966080 | tf_op jit(solution)/shard_map/gather_weights/all_gather | solution.py:41
  102.6 31.4 %copy-start.2 = (f32[4,2048]{1,0:T(4,128)S(1)}, f32[4,2048]{1,0:T(4,128)}, u32[]{:S(2)}) copy-start(f32[4,2048]{1,0:T(4,128)} %param.11) | copy-start | bytes 98308
  102.6 31.4 %copy-start.3 = (f32[4,2048]{1,0:T(4,128)S(1)}, f32[4,2048]{1,0:T(4,128)}, u32[]{:S(2)}) copy-start(f32[4,2048]{1,0:T(4,128)} %param.13) | copy-start | bytes 98308
  102.6 31.4 %copy-start.4 = (f32[4,2048]{1,0:T(4,128)S(1)}, f32[4,2048]{1,0:T(4,128)}, u32[]{:S(2)}) copy-start(f32[4,2048]{1,0:T(4,128)} %param.12) | copy-start | bytes 98308
  110.7 23.2 %all-to-all-start.4 = ((bf16[12,4,2048]{2,1,0:T(4,128)(2,1)}), bf16[12,4,2048]{2,1,0:T(4,128)(2,1)S(1)}, u32[]{:S(2)}, u32[]{:S(2)}) async-start(bf16[12,4,2048]{2,1,0:T(4,128)(2,1)} %gradient.1), calls=%async_computation.4 | async-start | bytes 393216 | tf_op jit(solution)/shard_map/gradient/all_to_all | solution.py:85
Sparse Core Ops, SparseCore 0:
  11.2 67.1 all-gather.2
Sparse Core Ops, SparseCore 1:
  97.5 28.7 all-gather.4

commit v5 on v4

--- a/solution.py
+++ b/solution.py
@@ -39,6 +39,7 @@
         pair = pair.transpose(2, 1, 0, 3, 4).reshape(2, n_zh * n_y * rows, width)
         last = spread(pair[0], "x", n_x)
         first = lax.all_gather(pair[1], "x", axis=0, tiled=False)
+
     def in_order(w):
         return w.reshape(n_x, n_zh, n_y * rows, width).transpose(1, 0, 2, 3).reshape(units, width)
 
@@ -50,7 +51,7 @@
             pick, hidden, (((1,), (1,)), ((), ())), preferred_element_type=F32
         ).astype(BF)
 
-    full_grads, last, hidden_t = lax.optimization_barrier((full_grads, last, hidden_t))
+    full_grads, hidden_t = lax.optimization_barrier((full_grads, hidden_t))
 
     with jax.named_scope("weights_of_tokens"):
         seg_row = segments[0]
@@ -59,16 +60,15 @@
         weight = tok_dev / DOCS / doc_len
         scaled = (full_grads.astype(F32) * weight[:, None]).astype(BF)
 
-    with jax.named_scope("hidden_grad"):
+    with jax.named_scope("gradient"):
+        grad_local = lax.dot_general(
+            hidden_t, scaled, (((1,), (0,)), ((), ())), preferred_element_type=F32
+        ).astype(BF)
+        grad_local, last = lax.optimization_barrier((grad_local, last))
         hidden_grad = lax.dot_general(
             scaled, in_order(last), (((1,), (1,)), ((), ())), preferred_element_type=F32
         )
         hidden_grad = hidden_grad.astype(BF)
-
-    with jax.named_scope("gradient"):
-        grad_local = lax.dot_general(
-            hidden_t, scaled, (((1,), (0,)), ((), ())), preferred_element_type=F32
-        ).astype(BF)
         parts = lax.all_to_all(
             grad_local.reshape(n_x * n_yl, units // (n_x * n_yl), width), ("x", "yl"), 0, 0
         )

time: 144 us -> 145 us (level)
  starting transfers between devices: 18.7 us -> 23 us
  waiting for transfers between devices: 33.2 us -> 29.2 us
    all_to_all x1, waiting for transfers between devices: 14 us -> 0.01 us  [spread(): lax.all_to_all(jnp.broadcast_to(block[None], (size,) + block.shape), axes...]
    all_gather x1, waiting for transfers between devices: 0.01 us -> 9.19 us  [per_device(): full_grads = lax.all_gather(out_grad, ('zl', 'c'), axis=0, tiled=True)]
    all_to_all x1, starting transfers between devices: 8.3 us -> 12.5 us  [per_device(): parts = lax.all_to_all(part, ('zh', 'yh'), 0, 0)]
    all_gather x1, waiting for transfers between devices: 6.5 us -> 2.76 us  [per_device(): first = lax.all_gather(pair[1], 'x', axis=0, tiled=False)]
    all_to_all x1, waiting for transfers between devices: 4.9 us -> 7.8 us  [per_device(): parts = lax.all_to_all(part, ('zh', 'yh'), 0, 0)]
    all_to_all x1, waiting for transfers between devices: 7.09 us -> 8.79 us  [per_device(): lax.all_to_all(grad_local.reshape(n_x * n_yl, units // (n_x * n_yl), widt...]
  transfers between devices with their start and end apart: 5 -> 5, of which waited for: 4 -> 4; matrix products, arithmetic and copies ran while one was open for 11% -> 15% of each run, Pallas kernels for 1% -> 1%
where the time goes in v5:
time: 145 us; the launch traced here: 143 us
  blocking collectives  50.4 us (35%)
  waiting for transfers between devices  29.2 us (20%)
  starting transfers between devices  23 us (16%)
  between operations  16.3 us (11%)
  matrix products  11.3 us (8%)
  local copies, waits for them, and re-layouts  8.92 us (6%)
  other arithmetic  2.86 us (2%)
    all_to_all x2, blocking collectives, spread(): lax.all_to_all(jnp.broadcast_to(block[None], (size,) + block.shape), axes...  50.4 us
    all_to_all x1, starting transfers between devices, per_device(): parts = lax.all_to_all(part, ('zh', 'yh'), 0, 0)  12.5 us
    all_gather x1, waiting for transfers between devices, per_device(): full_grads = lax.all_gather(out_grad, ('zl', 'c'), axis=0, tiled=True)  9.19 us
    all_to_all x1, waiting for transfers between devices, per_device(): lax.all_to_all(grad_local.reshape(n_x * n_yl, units // (n_x * n_yl), widt...  8.79 us
    all_to_all x1, waiting for transfers between devices, per_device(): parts = lax.all_to_all(part, ('zh', 'yh'), 0, 0)  7.8 us
    all_to_all x1, starting transfers between devices, per_device(): lax.all_to_all(grad_local.reshape(n_x * n_yl, units // (n_x * n_yl), widt...  5.72 us
    dot_general x1, matrix products, per_device(): lax.dot_general(scaled, in_order(last), (((1,), (1,)), ((), ())), preferr...  5.44 us
    dot_general x1, matrix products, per_device(): lax.dot_general(hidden_t, scaled, (((1,), (0,)), ((), ())), preferred_ele...  5.25 us
  transfers between devices with their start and end apart: 5, of which 4 were waited for; matrix products, arithmetic and copies ran while one was open for 15% of the time, Pallas kernels for 1%

profile of v5, /device:TPU:6, one launch (start us, length us, event | category | flops | bytes accessed | tf_op | source)
XLA Modules:
  0.0 143.1 jit_solution(7383667803208908627)
XLA Ops:
  8.1 0.7 all-gather.3.cloned.1.call-update
  8.7 0.8 convert_bitcast_fusion
  9.5 0.7 pad_maximum_fusion
  10.3 21.8 %all_to_all.25 = bf16[3,2,4,2048]{3,2,1,0:T(4,128)(2,1)S(1)} all-to-all(bf16[3,2,4,2048]{3,2,1,0:T(4,128)(2,1)S(1)} %broadcast_in_dim.8), channel_id=1, replica_groups=mesh['zh'=3,'x'=4,'yh'=4,'yl'=2,'zl'=4,'c'=2] {'zh'}, dimensions={0} | all-to-all | bytes 196608 | tf_op jit(solution)/shard_map/gather_weights/all_to_all | solution.py:22
  32.2 0.4 broadcast_in_dim.9
  32.5 28.6 %all_to_all.26 = bf16[8,3,2,4,2048]{4,3,1,2,0:T(4,128)(2,1)S(1)} all-to-all(bf16[8,3,2,4,2048]{4,3,1,2,0:T(4,128)(2,1)S(1)} %broadcast_in_dim.9), channel_id=1, replica_groups=mesh['zh'=3,'x'=4,'yh'=4,'yl'=2,'zl'=4,'c'=2] {'yh','yl'}, dimensions={0} | all-to-all | bytes 1572864 | tf_op jit(solution)/shard_map/gather_weights/all_to_all | solution.py:22
  61.8 1.3 broadcast_in_dim.11
  63.1 4.8 %all-to-all-start.2 = ((bf16[4,96,2048]{2,1,0:T(8,128)(2,1)}), bf16[4,96,2048]{2,1,0:T(8,128)(2,1)S(1)}, u32[]{:S(2)}, u32[]{:S(2)}) async-start(bf16[4,96,2048]{2,1,0:T(8,128)(2,1)} %broadcast_in_dim.11), calls=%async_computation.2 | async-start | bytes 3145728 | tf_op jit(solution)/shard_map/gather_weights/all_to_all | solution.py:22
  68.0 0.5 convert_reduce_fusion
  68.6 0.6 convolution_convert_fusion.1
  69.2 9.2 %all-gather.3.cloned.1.call-done = bf16[1024,2048]{1,0:T(8,128)(2,1)} async-done(((bf16[128,2048]{1,0:T(8,128)(2,1)}), bf16[1024,2048]{1,0:T(8,128)(2,1)}) %all-gather.3.cloned.1.call-update) | async-done | bytes 4194320 | tf_op jit(solution)/shard_map/gather_grads/all_gather | solution.py:33
  78.4 5.2 %convolution_convert_fusion = bf16[384,2048]{1,0:T(8,128)(2,1)} fusion(bf16[384,1024]{1,0:T(8,128)(2,1)S(1)} %convolution_convert_fusion.1, bf16[1024,2048]{1,0:T(8,128)(2,1)} %all-gather.3.cloned.1.call-done, f32[1024]{0:T(1024)S(1)} %broadcast_divide_fusion), kind=kOutput, calls=%fused_computation.2 | convolution fusion | flops 1617690624 | bytes 6557696 | tf_op jit(solution)/shard_map/gradient/dot_general | solution.py:64
  83.7 1.1 copy-done.1
  84.8 5.7 %all-to-all-start.3 = ((bf16[8,48,2048]{2,1,0:T(8,128)(2,1)}), bf16[8,48,2048]{2,1,0:T(8,128)(2,1)S(1)}, u32[]{:S(2)}, u32[]{:S(2)}) async-start(bf16[8,48,2048]{2,1,0:T(8,128)(2,1)} %bitcast.20), calls=%async_computation.3 | async-start | bytes 3145728 | tf_op jit(solution)/shard_map/gradient/all_to_all | solution.py:72
  90.7 0.8 slice.12
  91.6 1.5 %copy.23 = bf16[3,4,32,2048]{3,2,1,0:T(8,128)(2,1)S(1)} copy(bf16[3,4,32,2048]{3,2,0,1:T(8,128)(2,1)} %bitcast.17) | data formatting | bytes 3145728 | tf_op jit(solution)/shard_map/gradient/transpose | solution.py:44
  93.1 5.4 %fusion.1 = bf16[1024,384]{1,0:T(8,128)(2,1)} fusion(bf16[384,2048]{1,0:T(8,128)(2,1)S(1)} %bitcast.22, bf16[1024,2048]{1,0:T(8,128)(2,1)} %all-gather.3.cloned.1.call-done, f32[1024]{0:T(1024)S(1)} %broadcast_divide_fusion), kind=kOutput, calls=%fused_computation.4 | convolution fusion | flops 1617297408 | bytes 6557696 | tf_op jit(solution)/shard_map/gradient/dot_general | solution.py:68
  98.5 8.8 %all-to-all-done.3.parts = bf16[8,48,2048]{2,1,0:T(8,128)(2,1)S(1)} async-done(((bf16[8,48,2048]{2,1,0:T(8,128)(2,1)}), bf16[8,48,2048]{2,1,0:T(8,128)(2,1)S(1)}, u32[]{:S(2)}, u32[]{:S(2)}) %all-to-all-start.3) | async-done | bytes 1572896 | tf_op jit(solution)/shard_map/gradient/all_to_all | solution.py:72
  107.3 1.0 gradient.1
  108.3 12.5 %all-to-all-start.4 = ((bf16[12,4,2048]{2,1,0:T(4,128)(2,1)}), bf16[12,4,2048]{2,1,0:T(4,128)(2,1)S(1)}, u32[]{:S(2)}, u32[]{:S(2)}) async-start(bf16[12,4,2048]{2,1,0:T(4,128)(2,1)} %gradient.1), calls=%async_computation.4 | async-start | bytes 393216 | tf_op jit(solution)/shard_map/gradient/all_to_all | solution.py:85
  121.6 2.8 %all-gather.5.cloned.1.call-done = bf16[4,96,2048]{2,1,0:T(8,128)(2,1)} async-done(((bf16[1,96,2048]{2,1,0:T(8,128)(2,1)}), bf16[4,96,2048]{2,1,0:T(8,128)(2,1)}) %all-gather.5.cloned.1.call-update) | async-done | bytes 1572880 | tf_op jit(solution)/shard_map/gather_weights/all_gather | solution.py:41
  124.3 2.7 %copy.25 = bf16[3,4,32,2048]{3,2,1,0:T(8,128)(2,1)} copy(bf16[3,4,32,2048]{3,2,0,1:T(8,128)(2,1)} %bitcast.19) | data formatting | bytes 3145728 | tf_op jit(solution)/shard_map/gradient/transpose | solution.py:44
  127.1 7.8 %all-to-all-done.4 = bf16[12,4,2048]{2,1,0:T(4,128)(2,1)S(1)} async-done(((bf16[12,4,2048]{2,1,0:T(4,128)(2,1)}), bf16[12,4,2048]{2,1,0:T(4,128)(2,1)S(1)}, u32[]{:S(2)}, u32[]{:S(2)}) %all-to-all-start.4) | async-done | bytes 196640 | tf_op jit(solution)/shard_map/gradient/all_to_all | solution.py:85
  135.0 0.7 multiply_subtract_fusion
  (25 shorter events, 1.2 us)
Async XLA Ops:
  8.0 60.6 %copy-start = (bf16[1024,384]{1,0:T(8,128)(2,1)S(1)}, bf16[1024,384]{1,0:T(8,128)(2,1)}, u32[]{:S(2)}) copy-start(bf16[1024,384]{1,0:T(8,128)(2,1)} %param.9) | copy-start | bytes 2359300
  8.0 70.4 %all-gather.3.cloned.1.call-start = ((), (), s32[]{:S(2)}) async-start(), calls=%async_computation.5 | async-start | bytes 4718592 | tf_op jit(solution)/shard_map/gather_grads/all_gather | solution.py:33
  61.2 6.9 %copy-start.5 = (s32[1,1024]{1,0:T(1,128)S(1)}, s32[1,1024]{1,0:T(1,128)}, u32[]{:S(2)}) copy-start(s32[1,1024]{1,0:T(1,128)} %param.10) | copy-start | bytes 12292
  63.1 20.5 %all-to-all-start.2 = ((bf16[4,96,2048]{2,1,0:T(8,128)(2,1)}), bf16[4,96,2048]{2,1,0:T(8,128)(2,1)S(1)}, u32[]{:S(2)}, u32[]{:S(2)}) async-start(bf16[4,96,2048]{2,1,0:T(8,128)(2,1)} %broadcast_in_dim.11), calls=%async_computation.2 | async-start | bytes 3145728 | tf_op jit(solution)/shard_map/gather_weights/all_to_all | solution.py:22
  83.7 1.1 copy-start.1
  84.8 22.5 %all-to-all-start.3 = ((bf16[8,48,2048]{2,1,0:T(8,128)(2,1)}), bf16[8,48,2048]{2,1,0:T(8,128)(2,1)S(1)}, u32[]{:S(2)}, u32[]{:S(2)}) async-start(bf16[8,48,2048]{2,1,0:T(8,128)(2,1)} %bitcast.20), calls=%async_computation.3 | async-start | bytes 3145728 | tf_op jit(solution)/shard_map/gradient/all_to_all | solution.py:72
  90.5 33.8 %all-gather.5.cloned.1.call-start = ((), (), s32[]{:S(2)}) async-start(), calls=%async_computation.6 | async-start | bytes 1966080 | tf_op jit(solution)/shard_map/gather_weights/all_gather | solution.py:41
  98.5 36.4 %copy-start.2 = (f32[4,2048]{1,0:T(4,128)S(1)}, f32[4,2048]{1,0:T(4,128)}, u32[]{:S(2)}) copy-start(f32[4,2048]{1,0:T(4,128)} %param.11) | copy-start | bytes 98308
  98.5 36.4 %copy-start.3 = (f32[4,2048]{1,0:T(4,128)S(1)}, f32[4,2048]{1,0:T(4,128)}, u32[]{:S(2)}) copy-start(f32[4,2048]{1,0:T(4,128)} %param.13) | copy-start | bytes 98308
  98.5 36.4 %copy-start.4 = (f32[4,2048]{1,0:T(4,128)S(1)}, f32[4,2048]{1,0:T(4,128)}, u32[]{:S(2)}) copy-start(f32[4,2048]{1,0:T(4,128)} %param.12) | copy-start | bytes 98308
  108.3 26.5 %all-to-all-start.4 = ((bf16[12,4,2048]{2,1,0:T(4,128)(2,1)}), bf16[12,4,2048]{2,1,0:T(4,128)(2,1)S(1)}, u32[]{:S(2)}, u32[]{:S(2)}) async-start(bf16[12,4,2048]{2,1,0:T(4,128)(2,1)} %gradient.1), calls=%async_computation.4 | async-start | bytes 393216 | tf_op jit(solution)/shard_map/gradient/all_to_all | solution.py:85
Sparse Core Ops, SparseCore 0:
  11.2 67.1 all-gather.2
Sparse Core Ops, SparseCore 1:
  93.4 30.9 all-gather.4
